TPU v7x, 32 devices: a whole 2x2x4 slice. The times are simulated.
32 devices in a mesh: wide: 8 (over z, y), slab: 4 (over x, core).
Axes of the slice: x: 2, y: 2, z: 4, core: 2. Of those that a mesh axis runs over, the one named last changes fastest.
Arguments:
- thermal_state: float32 [8, 64, 32, 1024], P('wide', 'slab'), may hold values from -5 to 5
- thermal_spreading_rate: bfloat16 [8, 64, 32, 1024], P('wide', 'slab'), may hold values from 0.5 to 1.5
- flow_speed_vector: bfloat16 [3, 8, 64, 32, 1024], P(None, 'wide', 'slab'), may hold values from -0.796875 to 0.796875
- interface_guess: float32 [8, 1024], P('wide', 'slab'), may hold values from -4 to 4
- partner_facing_rows: int32 [8, 1024], P('wide', 'slab'), may hold values from 0 to 1023, each once within a row
- mismatch_change_matrix: float32 [8, 1024, 128], P('wide', 'slab'), may hold values from -5 to 5
- output_change_matrix: float32 [8, 1024, 128], P('wide', 'slab'), may hold values from -1.8 to 1.8
Outputs:
- temperature_out: float32 [8, 64, 32, 1024], P('wide', 'slab')
- updated_interface_guess: float32 [8, 1024], P('wide', 'slab')
- unitary_basis_factor: float32 [8, 1024, 128], P('wide', 'slab')
Inputs may be any that keep to these rules, and one draw needn't show every extreme that they name: `partner_facing_rows`: each partition's rows of matching are a permutation of its partner's interface rows.
All inputs are finite; a program needn't handle non-finite values.
Results may differ from a plain program's by a relative error of at most 0.0003.
Values may be sent and summed in bfloat16 or wider, within the bound.
A program may use at most 64 MiB of HBM per device.

v0:
```python
import math

import jax
import jax.numpy as jnp
from jax import lax
from jax.sharding import PartitionSpec as P

INTERFACE_STRIP = 64
SWEEPS = 4


STEP_SIZE = 0.11


def padded(cells, sides, width):
    for axis, dim in sides:
        count = lax.axis_size(axis)
        ends = count - 1
        head = lax.slice_in_dim(cells, 0, width, axis=dim)
        tail = lax.slice_in_dim(cells, cells.shape[dim] - width, cells.shape[dim], axis=dim)
        cells = jnp.concatenate(
            [
                lax.ppermute(tail, axis, [(i, (i + 1) % count) for i in range(ends)]),
                cells,
                lax.ppermute(head, axis, [((i + 1) % count, i) for i in range(ends)]),
            ],
            axis=dim,
        )
    return cells


def partner(value, axis, stride):
    mask = 2**stride
    pairs = [(source, source ^ mask) for source in range(lax.axis_size(axis))]
    return lax.ppermute(value, axis, pairs)


def surround_wrapper(block_rows, mirror_layer):
    bottom = jnp.zeros((block_rows.shape[0], 1, block_rows.shape[2]), block_rows.dtype)
    stacked = jnp.concatenate([bottom, block_rows, mirror_layer[:, None, :]], axis=1)
    return jnp.pad(stacked, ((0, 0), (0, 0), (1, 1)))


def march_forward(bordered_array, diffuse_subdomain, subdomain_flow_speed):
    centre = bordered_array[1:-1, 1:-1, 1:-1]
    plus_first = bordered_array[2:, 1:-1, 1:-1]
    minus_first = bordered_array[:-2, 1:-1, 1:-1]
    plus_second = bordered_array[1:-1, 2:, 1:-1]
    minus_second = bordered_array[1:-1, :-2, 1:-1]
    plus_third = bordered_array[1:-1, 1:-1, 2:]
    minus_third = bordered_array[1:-1, 1:-1, :-2]
    spread = (
        plus_first
        + minus_first
        + plus_second
        + minus_second
        + plus_third
        + minus_third
        - 6.0 * centre
    )
    carried = 0.5 * (
        subdomain_flow_speed[0].astype(jnp.float32) * (plus_first - minus_first)
        + subdomain_flow_speed[1].astype(jnp.float32) * (plus_second - minus_second)
        + subdomain_flow_speed[2].astype(jnp.float32) * (plus_third - minus_third)
    )
    return centre + STEP_SIZE * (diffuse_subdomain.astype(jnp.float32) * spread - carried)


def shards(
    thermal_state,
    thermal_spreading_rate,
    flow_speed_vector,
    interface_guess,
    partner_facing_rows,
    mismatch_change_matrix,
    output_change_matrix,
):
    subdomain_thermal_state = thermal_state[0]
    diffuse_subdomain = thermal_spreading_rate[0]
    subdomain_flow_speed = flow_speed_vector[:, 0]
    layer_stack = subdomain_thermal_state.shape[0]
    vertical_extent = subdomain_thermal_state.shape[1]
    rows_dev = interface_guess.shape[1]
    mirror_layer = jnp.repeat(interface_guess[0].reshape(layer_stack, -1), INTERFACE_STRIP, axis=1)
    panel = mismatch_change_matrix[0]
    gram_local = lax.dot_general(
        panel,
        panel,
        (((0,), (0,)), ((), ())),
        precision=lax.Precision.HIGHEST,
        preferred_element_type=jnp.float32,
    )
    ghost_padded = jnp.pad(mirror_layer, ((1, 1), (0, 0)))
    for sweep in range(SWEEPS):
        widened_array = padded(subdomain_thermal_state, (("slab", 0),), 1)
        subdomain_thermal_state = march_forward(
            surround_wrapper(widened_array, ghost_padded), diffuse_subdomain, subdomain_flow_speed
        )
    face_means = jnp.mean(
        subdomain_thermal_state[:, vertical_extent - 1, :].reshape(
            layer_stack, -1, INTERFACE_STRIP
        ),
        axis=2,
    )
    face_means = face_means.reshape(1, rows_dev)
    top_bit = lax.axis_size("wide").bit_length() - 2
    partner_own = partner(face_means, "wide", top_bit)
    partner_all = lax.all_gather(partner_own, "slab", axis=1, tiled=True)
    tilde = jnp.take(partner_all[0], partner_facing_rows[0], axis=0)
    resid = tilde - interface_guess[0]
    proj_local = jnp.dot(
        resid, panel, precision=lax.Precision.HIGHEST, preferred_element_type=jnp.float32
    )
    gram_matrix, projection = lax.psum((gram_local, proj_local), ("wide", "slab"))
    lower_factor = jnp.linalg.cholesky(gram_matrix)
    half_solve = lax.linalg.triangular_solve(
        lower_factor, projection[:, None], left_side=True, lower=True
    )
    coefficients = -lax.linalg.triangular_solve(
        lower_factor, half_solve, left_side=True, lower=True, transpose_a=True
    )[:, 0]
    update = jnp.dot(
        output_change_matrix[0],
        coefficients,
        precision=lax.Precision.HIGHEST,
        preferred_element_type=jnp.float32,
    )
    updated_interface_guess = tilde + update
    total_rows = rows_dev * lax.axis_size("slab") * lax.axis_size("wide")
    scaled = lax.linalg.triangular_solve(
        lower_factor, panel, left_side=False, lower=True, transpose_a=True
    )
    unitary_basis_factor = math.sqrt(total_rows) * scaled
    return (
        subdomain_thermal_state[None],
        updated_interface_guess[None],
        unitary_basis_factor[None],
    )


def solution(mesh):
    return jax.shard_map(
        shards,
        mesh=mesh,
        in_specs=(
            P("wide", "slab", None, None),
            P("wide", "slab", None, None),
            P(None, "wide", "slab", None, None),
            P("wide", "slab"),
            P("wide", "slab"),
            P("wide", "slab", None),
            P("wide", "slab", None),
        ),
        out_specs=(P("wide", "slab", None, None), P("wide", "slab"), P("wide", "slab", None)),
        check_vma=False,
    )
```

profile of v0, /device:TPU:0, one launch (start us, length us, event | category | flops | bytes accessed | tf_op | source)
XLA Modules:
  0.0 275.5 jit_solution(6973544416327719661)
XLA Ops:
  7.2 1.0 slice_bitcast_fusion
  8.2 1.3 collective-permute-start
  9.5 3.0 %collective-permute-start.1 = (f32[1,32,1024]{2,1,0:T(8,128)S(1)}, f32[1,32,1024]{2,1,0:T(8,128)S(1)}, u32[]{:S(2)}, u32[]{:S(2)}) collective-permute-start(f32[1,32,1024]{2,1,0:T(8,128)S(1)} %get-tuple-element.15), channel_id=1, source_target_pairs={{0,1},{1,2},{2,3},{4,5},{5,6},{6,7},{8,9},{9,10},{10,11},{12,13},{... | collective-permute-start | bytes 393224 | tf_op jit(solution)/shard_map/ppermute | solution.py:23
  12.6 1.0 fusion.39
  13.6 0.7 compare_select_fusion.1
  14.3 0.5 broadcast.243
  14.8 1.3 reduce.11
  16.6 117.9 %all-reduce.11.cloned.1.call-done = f32[128,128]{0,1:T(8,128)} async-done(((f32[128,128]{0,1:T(8,128)}), f32[128,128]{0,1:T(8,128)}) %all-reduce.11.cloned.1.call-update) | async-done | bytes 65552 | tf_op jit(solution)/shard_map/psum | solution.py:114
  134.5 0.9 copy.14
  135.4 0.6 copy-done.10
  136.1 2.3 pad_maximum_fusion.3
  138.3 0.3 copy-done.1
  138.6 0.3 copy-done.6
  138.9 7.0 %fusion.2 = f32[16,32,1024]{2,1,0:T(8,128)S(1)} fusion(f32[16,32,1024]{2,1,0:T(8,128)} %bitcast.90, f32[18,34,1024]{2,1,0:T(8,128)S(1)} %pad_maximum_fusion.3, f32[1,32,1024]{2,1,0:T(8,128)S(1)} %collective-permute-done, f32[1,32,1024]{2,1,0:T(8,128)S(1)} %copy-done.11, f32[18,1,1024]{2,1,0:T(1,128)S(1)} %broadcast_in_dim.30, ...), kind=kLoop, calls=%fused_computation.35 | loop fusion | flops 18874368 | bytes 11231232 | tf_op jit(solution)/shard_map/add | solution.py:66
  145.9 1.3 copy-done.4
  147.3 0.7 fusion.61
  148.0 1.3 collective-permute-start.2
  149.3 4.8 %collective-permute-start.3 = (f32[1,32,1024]{2,1,0:T(8,128)}, f32[1,32,1024]{2,1,0:T(8,128)}, u32[]{:S(2)}, u32[]{:S(2)}) collective-permute-start(f32[1,32,1024]{2,1,0:T(8,128)} %get-tuple-element.13), channel_id=1, source_target_pairs={{0,1},{1,2},{2,3},{4,5},{5,6},{6,7},{8,9},{9,10},{10,11},{12,13},{... | collective-permute-start | bytes 393224 | tf_op jit(solution)/shard_map/ppermute | solution.py:23
  154.0 0.6 fusion.45
  154.7 12.5 %cholesky.16 = f32[128,128]{1,0:T(8,128)S(1)} custom-call(f32[128,128]{1,0:T(8,128)} %fusion.45), custom_call_target="Cholesky" | custom-call | tf_op jit(solution)/shard_map/jit(cholesky)/cholesky | solution.py:115
  167.3 2.3 pad_maximum_fusion.2
  169.6 0.2 copy-done.7
  169.8 4.6 %fusion.5 = f32[16,32,1024]{2,1,0:T(8,128)S(1)} fusion(f32[16,32,1024]{2,1,0:T(8,128)S(1)} %copy-done.5, f32[18,34,1024]{2,1,0:T(8,128)S(1)} %pad_maximum_fusion.2, f32[1,32,1024]{2,1,0:T(8,128)S(1)} %collective-permute-done.2, f32[1,32,1024]{2,1,0:T(8,128)} %collective-permute-done.3, f32[18,1,1024]{2,1,0:T(1,128)S(1)} %broadcast_in_dim.30, ...), kind=kLoop, calls=%fused_computation.38 | loop fusion | flops 18874368 | bytes 11231232 | tf_op jit(solution)/shard_map/add | solution.py:66
  174.5 1.3 collective-permute-start.4
  175.8 3.8 %collective-permute-start.5 = (f32[1,32,1024]{2,1,0:T(8,128)S(1)}, f32[1,32,1024]{2,1,0:T(8,128)S(1)}, u32[]{:S(2)}, u32[]{:S(2)}) collective-permute-start(f32[1,32,1024]{2,1,0:T(8,128)S(1)} %get-tuple-element.11), channel_id=1, source_target_pairs={{0,1},{1,2},{2,3},{4,5},{5,6},{6,7},{8,9},{9,10},{10,11},{12,13},{... | collective-permute-start | bytes 393224 | tf_op jit(solution)/shard_map/ppermute | solution.py:23
  179.6 0.6 compare_reduce_fusion
  180.4 0.7 pad_maximum_fusion.1
  181.1 5.4 %fusion.8 = f32[16,32,1024]{2,1,0:T(8,128)S(1)} fusion(f32[16,32,1024]{2,1,0:T(8,128)S(1)} %fusion.5, f32[18,34,1024]{2,1,0:T(8,128)S(1)} %pad_maximum_fusion.1, f32[1,32,1024]{2,1,0:T(8,128)S(1)} %collective-permute-done.4, f32[1,32,1024]{2,1,0:T(8,128)S(1)} %collective-permute-done.5, f32[18,1,1024]{2,1,0:T(1,128)S(1)} %broadcast_in_dim.30, ...), kind=kLoop, calls=%fused_computation.41 | loop fusion | flops 18874368 | bytes 11231232 | tf_op jit(solution)/shard_map/add | solution.py:66
  186.5 1.3 copy-done.2
  187.8 0.7 fusion.59
  188.5 1.3 collective-permute-start.6
  189.8 5.9 %collective-permute-start.7 = (f32[1,32,1024]{2,1,0:T(8,128)}, f32[1,32,1024]{2,1,0:T(8,128)}, u32[]{:S(2)}, u32[]{:S(2)}) collective-permute-start(f32[1,32,1024]{2,1,0:T(8,128)} %get-tuple-element.9), channel_id=1, source_target_pairs={{0,1},{1,2},{2,3},{4,5},{5,6},{6,7},{8,9},{9,10},{10,11},{12,13},{... | collective-permute-start | bytes 393224 | tf_op jit(solution)/shard_map/ppermute | solution.py:23
  195.7 1.3 fusion.41
  196.9 10.6 %custom-call.10 = f32[1,128,128]{1,2,0:T(8,128)S(1)} custom-call(f32[1,128,128]{2,1,0:T(8,128)} %fusion.41), custom_call_target="InvertDiagBlocksLowerTriangular" | custom-call | tf_op jit(solution)/shard_map/triangular_solve | solution.py:119
  207.6 2.3 pad_maximum_fusion
  209.9 0.2 copy-done.8
  210.1 4.6 %fusion.11 = f32[16,32,1024]{2,1,0:T(8,128)S(1)} fusion(f32[16,32,1024]{2,1,0:T(8,128)S(1)} %copy-done.3, f32[18,34,1024]{2,1,0:T(8,128)S(1)} %pad_maximum_fusion, f32[1,32,1024]{2,1,0:T(8,128)S(1)} %collective-permute-done.6, f32[1,32,1024]{2,1,0:T(8,128)} %collective-permute-done.7, f32[18,1,1024]{2,1,0:T(1,128)S(1)} %broadcast_in_dim.30, ...), kind=kLoop, calls=%fused_computation.44 | loop fusion | flops 18874368 | bytes 11231232 | tf_op jit(solution)/shard_map/add | solution.py:66
  214.8 1.3 copy-done.9
  216.6 1.3 collective-permute-start.8
  217.9 0.3 fusion.32
  218.2 0.8 copy.15
  219.0 2.1 collective-permute-done.8
  221.1 5.2 %all_gather.3 = f32[1,1024]{1,0:T(1,128)S(1)} all-gather(f32[1,256]{1,0:T(1,128)S(1)} %collective-permute-done.8), channel_id=1, replica_groups=mesh['wide'=8,'slab'=4] {'slab'}, dimensions={1}, use_global_device_ids=true | all-gather | bytes 5120 | tf_op jit(solution)/shard_map/all_gather | solution.py:108
  226.3 1.4 gather_fusion
  227.9 39.6 %psum.15 = f32[128]{0:T(128)S(1)} all-reduce(f32[128]{0:T(128)S(1)} %convolution_bitcast_fusion.2), channel_id=1, replica_groups=mesh['wide'=8,'slab'=4] {'wide','slab'}, use_global_device_ids=true, to_apply=%region_4.5 | all-reduce | flops 128 | bytes 1024 | tf_op jit(solution)/shard_map/psum | solution.py:114
  267.7 0.2 fusion.34
  267.8 0.2 fusion.35
  268.1 0.6 fusion.46
  (54 shorter events, 1.4 us)
Async XLA Ops:
  7.2 5.4 %copy-start = (f32[1,256,128]{2,1,0:T(8,128)S(1)}, f32[1,256,128]{2,1,0:T(8,128)}, u32[]{:S(2)}) copy-start(f32[1,256,128]{2,1,0:T(8,128)} %param.12) | copy-start | bytes 393220
  7.2 127.3 %all-reduce.11.cloned.1.call-start = ((), (), s32[]{:S(2)}) async-start(), calls=%async_computation | async-start | bytes 131072 | tf_op jit(solution)/shard_map/psum | solution.py:114
  8.2 127.1 %collective-permute-start = (f32[1,32,1024]{2,1,0:T(8,128)S(1)}, f32[1,32,1024]{2,1,0:T(8,128)S(1)}, u32[]{:S(2)}, u32[]{:S(2)}) collective-permute-start(f32[1,32,1024]{2,1,0:T(8,128)S(1)} %get-tuple-element.16), channel_id=1, source_target_pairs={{1,0},{2,1},{3,2},{5,4},{6,5},{7,6},{9,8},{10,9},{11,10},{13,12},{... | collective-permute-start | bytes 393224 | tf_op jit(solution)/shard_map/ppermute | solution.py:25
  9.5 125.9 %collective-permute-start.1 = (f32[1,32,1024]{2,1,0:T(8,128)S(1)}, f32[1,32,1024]{2,1,0:T(8,128)S(1)}, u32[]{:S(2)}, u32[]{:S(2)}) collective-permute-start(f32[1,32,1024]{2,1,0:T(8,128)S(1)} %get-tuple-element.15), channel_id=1, source_target_pairs={{0,1},{1,2},{2,3},{4,5},{5,6},{6,7},{8,9},{9,10},{10,11},{12,13},{... | collective-permute-start | bytes 393224 | tf_op jit(solution)/shard_map/ppermute | solution.py:23
  135.4 0.7 copy-start.10
  136.1 2.6 copy-start.1
  136.1 2.8 %copy-start.6 = (bf16[1,16,32,1024]{3,2,1,0:T(8,128)(2,1)S(1)}, bf16[1,16,32,1024]{3,2,1,0:T(8,128)(2,1)}, u32[]{:S(2)}) copy-start(bf16[1,16,32,1024]{3,2,1,0:T(8,128)(2,1)} %param.8) | copy-start | bytes 3145732
  136.1 2.8 %copy-start.11 = (f32[1,32,1024]{2,1,0:T(8,128)S(1)}, f32[1,32,1024]{2,1,0:T(8,128)}, u32[]{:S(2)}) copy-start(f32[1,32,1024]{2,1,0:T(8,128)} %copy-done.10) | copy-start | bytes 393220
  138.9 15.1 %copy-start.12 = (f32[128,128]{0,1:T(8,128)S(1)}, f32[128,128]{0,1:T(8,128)}, u32[]{:S(2)}) copy-start(f32[128,128]{0,1:T(8,128)} %all-reduce.11.cloned.1.call-done) | copy-start | bytes 196612
  145.9 1.3 copy-start.4
  148.0 19.3 %collective-permute-start.2 = (f32[1,32,1024]{2,1,0:T(8,128)}, f32[1,32,1024]{2,1,0:T(8,128)S(1)}, u32[]{:S(2)}, u32[]{:S(2)}) collective-permute-start(f32[1,32,1024]{2,1,0:T(8,128)} %get-tuple-element.14), channel_id=1, source_target_pairs={{1,0},{2,1},{3,2},{5,4},{6,5},{7,6},{9,8},{10,9},{11,10},{13,12},{... | collective-permute-start | bytes 393224 | tf_op jit(solution)/shard_map/ppermute | solution.py:25
  149.3 18.0 %collective-permute-start.3 = (f32[1,32,1024]{2,1,0:T(8,128)}, f32[1,32,1024]{2,1,0:T(8,128)}, u32[]{:S(2)}, u32[]{:S(2)}) collective-permute-start(f32[1,32,1024]{2,1,0:T(8,128)} %get-tuple-element.13), channel_id=1, source_target_pairs={{0,1},{1,2},{2,3},{4,5},{5,6},{6,7},{8,9},{9,10},{10,11},{12,13},{... | collective-permute-start | bytes 393224 | tf_op jit(solution)/shard_map/ppermute | solution.py:23
  167.2 12.4 %copy-start.13 = (f32[128,128]{1,0:T(8,128)}, f32[128,128]{1,0:T(8,128)S(1)}, u32[]{:S(2)}) copy-start(f32[128,128]{1,0:T(8,128)S(1)} %cholesky.16) | copy-start | bytes 196612
  167.2 2.3 copy-start.5
  167.2 2.5 copy-start.7
  174.5 5.8 %collective-permute-start.4 = (f32[1,32,1024]{2,1,0:T(8,128)S(1)}, f32[1,32,1024]{2,1,0:T(8,128)S(1)}, u32[]{:S(2)}, u32[]{:S(2)}) collective-permute-start(f32[1,32,1024]{2,1,0:T(8,128)S(1)} %get-tuple-element.12), channel_id=1, source_target_pairs={{1,0},{2,1},{3,2},{5,4},{6,5},{7,6},{9,8},{10,9},{11,10},{13,12},{... | collective-permute-start | bytes 393224 | tf_op jit(solution)/shard_map/ppermute | solution.py:25
  175.8 4.6 %collective-permute-start.5 = (f32[1,32,1024]{2,1,0:T(8,128)S(1)}, f32[1,32,1024]{2,1,0:T(8,128)S(1)}, u32[]{:S(2)}, u32[]{:S(2)}) collective-permute-start(f32[1,32,1024]{2,1,0:T(8,128)S(1)} %get-tuple-element.11), channel_id=1, source_target_pairs={{0,1},{1,2},{2,3},{4,5},{5,6},{6,7},{8,9},{9,10},{10,11},{12,13},{... | collective-permute-start | bytes 393224 | tf_op jit(solution)/shard_map/ppermute | solution.py:23
  181.0 14.6 %copy-start.14 = (f32[128,128]{1,0:T(8,128)S(1)}, f32[128,128]{1,0:T(8,128)}, u32[]{:S(2)}) copy-start(f32[128,128]{1,0:T(8,128)} %copy-done.13) | copy-start | bytes 196612
  186.5 1.3 copy-start.2
  188.5 19.1 %collective-permute-start.6 = (f32[1,32,1024]{2,1,0:T(8,128)}, f32[1,32,1024]{2,1,0:T(8,128)S(1)}, u32[]{:S(2)}, u32[]{:S(2)}) collective-permute-start(f32[1,32,1024]{2,1,0:T(8,128)} %get-tuple-element.10), channel_id=1, source_target_pairs={{1,0},{2,1},{3,2},{5,4},{6,5},{7,6},{9,8},{10,9},{11,10},{13,12},{... | collective-permute-start | bytes 393224 | tf_op jit(solution)/shard_map/ppermute | solution.py:25
  189.8 17.8 %collective-permute-start.7 = (f32[1,32,1024]{2,1,0:T(8,128)}, f32[1,32,1024]{2,1,0:T(8,128)}, u32[]{:S(2)}, u32[]{:S(2)}) collective-permute-start(f32[1,32,1024]{2,1,0:T(8,128)} %get-tuple-element.9), channel_id=1, source_target_pairs={{0,1},{1,2},{2,3},{4,5},{5,6},{6,7},{8,9},{9,10},{10,11},{12,13},{... | collective-permute-start | bytes 393224 | tf_op jit(solution)/shard_map/ppermute | solution.py:23
  207.6 2.3 copy-start.3
  207.6 2.5 copy-start.8
  214.8 1.3 copy-start.9
  216.1 11.6 %copy-start.16 = (s32[1,256]{1,0:T(1,128)S(1)}, s32[1,256]{1,0:T(1,128)}, u32[]{:S(2)}) copy-start(s32[1,256]{1,0:T(1,128)} %param.11) | copy-start | bytes 3076
  216.1 11.6 %copy-start.17 = (f32[1,256]{1,0:T(1,128)S(1)}, f32[1,256]{1,0:T(1,128)}, u32[]{:S(2)}) copy-start(f32[1,256]{1,0:T(1,128)} %param.10) | copy-start | bytes 3076
  216.1 51.7 %copy-start.15 = (f32[1,256,128]{2,1,0:T(8,128)S(1)}, f32[1,256,128]{2,1,0:T(8,128)}, u32[]{:S(2)}) copy-start(f32[1,256,128]{2,1,0:T(8,128)} %param.13) | copy-start | bytes 393220
  216.6 4.5 %collective-permute-start.8 = (f32[1,256]{1,0:T(1,128)S(1)}, f32[1,256]{1,0:T(1,128)S(1)}, u32[]{:S(2)}, u32[]{:S(2)}) collective-permute-start(f32[1,256]{1,0:T(1,128)S(1)} %div.18), channel_id=1, source_target_pairs={{0,16},{4,20},{8,24},{12,28},{16,0},{20,4},{24,8},{28,12},{1,17},{... | collective-permute-start | bytes 3080 | tf_op jit(solution)/shard_map/ppermute | solution.py:35
Sparse Core Ops, SparseCore 0:
  14.2 120.2 all-reduce.10
where the time goes:
time: 276 us
  waiting for transfers between devices  120 us (43%)
  other arithmetic  57.7 us (21%)
  blocking collectives  44.9 us (16%)
  starting transfers between devices  24 us (9%)
  between operations  14.4 us (5%)
  local copies, waits for them, and re-layouts  12.3 us (4%)
    psum x1, waiting for transfers between devices, shards(): lax.psum((gram_local, proj_local), ('wide', 'slab'))  118 us
    psum x1, blocking collectives, shards(): lax.psum((gram_local, proj_local), ('wide', 'slab'))  39.6 us
    add x4, other arithmetic, march_forward(): centre + STEP_SIZE * (diffuse_subdomain.astype(jnp.float32) * spread - ca...  21.7 us
    ppermute x4, starting transfers between devices, padded(): lax.ppermute(tail, axis, [(i, (i + 1) % count) for i in range(ends)])  17.5 us
    another operation x3, other arithmetic, shards(): lower_factor = jnp.linalg.cholesky(gram_matrix)  13.2 us
    another operation x2, other arithmetic, shards(): lax.linalg.triangular_solve(lower_factor, half_solve, left_side=True, low...  11.9 us
    concatenate x4, other arithmetic, surround_wrapper(): jnp.concatenate([bottom, block_rows, mirror_layer[:, None, :]], axis=1)  7.47 us
    unnamed x38, local copies, waits for them, and re-layouts  6.89 us
  transfers between devices with their start and end apart: 10, of which 3 were waited for; matrix products, arithmetic and copies ran while one was open for 11% of the time, Pallas kernels for 0%

commit v1 on v0

v1 whole, which is shorter than its diff:
```python
import functools
import math

import jax
import jax.numpy as jnp
from jax import lax
from jax.experimental import pallas as pl
from jax.experimental.pallas import tpu as pltpu
from jax.sharding import PartitionSpec as P

INTERFACE_STRIP = 64
SWEEPS = 4
STEP_SIZE = 0.11
TOP = 8
MESH = pl.DeviceIdType.MESH
HIGHEST = lax.Precision.HIGHEST
F32 = jnp.float32
BF16 = jnp.bfloat16


def iota(shape, dim):
    return lax.broadcasted_iota(jnp.int32, shape, dim)


def split3(value):
    hi = value.astype(BF16).astype(F32)
    rest = value - hi
    mid = rest.astype(BF16).astype(F32)
    return hi, mid, rest - mid


def march_rows(centre, plus_first, minus_first, plus_second, minus_second, rate, flow):
    depth = centre.shape[1]
    lane = iota((centre.shape[0], 128), 1)
    right = pltpu.roll(centre, depth - 1, 1)
    left = pltpu.roll(centre, 1, 1)
    plus_third = jnp.concatenate(
        [right[:, : depth - 128], jnp.where(lane == 127, 0.0, right[:, depth - 128 :])], axis=1
    )
    minus_third = jnp.concatenate(
        [jnp.where(lane == 0, 0.0, left[:, :128]), left[:, 128:]], axis=1
    )
    spread = (
        (plus_first + minus_first)
        + (plus_second + minus_second)
        + (plus_third + minus_third)
        - 6.0 * centre
    )
    carried = (
        flow[0].astype(F32) * (plus_first - minus_first)
        + flow[1].astype(F32) * (plus_second - minus_second)
        + flow[2].astype(F32) * (plus_third - minus_third)
    )
    return centre + (STEP_SIZE * rate.astype(F32) * spread - (0.5 * STEP_SIZE) * carried)


def eliminate(strips, first, last, blocks):
    lane = iota((8, 128), 1)
    row = iota((8, 128), 0)

    def block(b, strips):
        strips = list(strips)
        for i in range(8):
            columns = [jnp.broadcast_to(s[:, i : i + 1], (8, 128)) for s in strips]
            pivot = jnp.broadcast_to(columns[0][i : i + 1, :], (8, 128))
            inverse = 1.0 / pivot
            along = jnp.broadcast_to(strips[0][i : i + 1, :], (8, 128))
            scaled = jnp.where(lane == i, inverse, along * inverse)
            below = row > i
            strips[0] = jnp.where((lane == i) & below, 0.0, strips[0]) - jnp.where(
                below, columns[0], 0.0
            ) * scaled
            for t in range(1, blocks):
                strips[t] = jnp.where(lane == i, 0.0, strips[t]) - columns[t] * scaled
        kept = ((lane < 8) & (lane <= row)) | (lane >= 8 * (blocks - b))
        strips[0] = jnp.where(kept, strips[0], 0.0)
        strips = [pltpu.roll(s, 128 - 8, 1) for s in strips]
        return tuple(strips[1:] + strips[:1])

    return lax.fori_loop(first, last, block, tuple(strips))


def kernel(
    n_wide,
    n_slab,
    total_rows,
    state_hbm,
    rate_hbm,
    flow_hbm,
    guess_ref,
    rows_ref,
    panel_ref,
    output_ref,
    final_hbm,
    updated_ref,
    basis_ref,
    cells,
    halo,
    rate,
    flow,
    spread_map,
    pick_map,
    gram_own,
    gram_scatter,
    gram_sum,
    gram_wide,
    gram_part,
    gram_full,
    elim,
    face_own,
    face_all,
    proj_own,
    proj_slab,
    proj_sum,
    proj_wide,
    load_sem,
    store_sem,
    halo_send,
    halo_recv,
    slab_send,
    slab_recv,
    wide_send,
    wide_recv,
    face_send,
    face_recv,
):
    layers, depth = cells.shape[1], cells.shape[3]
    height = rate.shape[1]
    cols = panel_ref.shape[1]
    rows_dev = guess_ref.shape[1]
    per_layer = depth // INTERFACE_STRIP
    part_rows = cols // n_slab
    me_w, me_s = lax.axis_index("wide"), lax.axis_index("slab")
    across = lax.rem(me_w + n_wide // 2, n_wide)

    def slab_peer(k):
        return lax.rem(me_s + k, n_slab)

    def wide_peer(k):
        return lax.rem(me_w + k, n_wide)

    quarter = layers // 4
    loads = {}
    for g in (0, 3, 1, 2):
        planes = pl.ds(g * quarter, quarter)
        loads[g] = [
            pltpu.make_async_copy(
                state_hbm.at[0, planes], cells.at[0, planes, pl.ds(TOP, height)], load_sem.at[g, 0]
            ),
            pltpu.make_async_copy(rate_hbm.at[0, planes], rate.at[planes], load_sem.at[g, 1]),
            pltpu.make_async_copy(
                flow_hbm.at[:, 0, planes], flow.at[:, planes], load_sem.at[g, 2]
            ),
        ]
        for c in loads[g]:
            c.start()

    zeros = jnp.zeros((height, depth), F32)
    for side in range(2):

        @pl.when(me_s == side * (n_slab - 1))
        def _():
            for sweep in range(SWEEPS):
                halo[sweep, side] = zeros

    barrier = pltpu.get_barrier_semaphore()
    peers = (
        [(me_w, slab_peer(k)) for k in range(1, n_slab)]
        + [(wide_peer(k), me_s) for k in range(1, n_wide)]
        + [(across, slab_peer(k)) for k in range(1, n_slab)]
    )
    for peer in peers:
        pl.semaphore_signal(barrier, inc=1, device_id=peer, device_id_type=MESH)
    pl.semaphore_wait(barrier, len(peers))

    def halo_copies(sweep, low, high):
        down = pltpu.make_async_remote_copy(
            src_ref=low,
            dst_ref=halo.at[sweep, 1],
            send_sem=halo_send.at[sweep, 0],
            recv_sem=halo_recv.at[sweep, 1],
            device_id=(me_w, lax.max(me_s - 1, 0)),
            device_id_type=MESH,
        )
        up = pltpu.make_async_remote_copy(
            src_ref=high,
            dst_ref=halo.at[sweep, 0],
            send_sem=halo_send.at[sweep, 1],
            recv_sem=halo_recv.at[sweep, 0],
            device_id=(me_w, lax.min(me_s + 1, n_slab - 1)),
            device_id_type=MESH,
        )
        return down, up

    def send_halo(copies):
        @pl.when(me_s > 0)
        def _():
            copies[0].start()

        @pl.when(me_s < n_slab - 1)
        def _():
            copies[1].start()

    def wait_halo(copies):
        @pl.when(me_s > 0)
        def _():
            copies[0].wait_send()
            copies[1].wait_recv()

        @pl.when(me_s < n_slab - 1)
        def _():
            copies[1].wait_send()
            copies[0].wait_recv()

    copies = halo_copies(0, state_hbm.at[0, 0], state_hbm.at[0, layers - 1])
    send_halo(copies)

    def slab_exchange(source, target, phase):
        out = []
        for k in range(1, n_slab):
            c = pltpu.make_async_remote_copy(
                src_ref=source(slab_peer(k)),
                dst_ref=target.at[me_s],
                send_sem=slab_send.at[phase, k],
                recv_sem=slab_recv.at[phase, k],
                device_id=(me_w, slab_peer(k)),
                device_id_type=MESH,
            )
            c.start()
            out.append(c)
        return out

    def wide_exchange(source, target, phase):
        out = []
        for k in range(1, n_wide):
            c = pltpu.make_async_remote_copy(
                src_ref=source,
                dst_ref=target.at[me_w],
                send_sem=wide_send.at[phase, k],
                recv_sem=wide_recv.at[phase, k],
                device_id=(wide_peer(k), me_s),
                device_id_type=MESH,
            )
            c.start()
            out.append(c)
        return out

    def finish(exchange):
        for c in exchange:
            c.wait()

    def summed(ref, count):
        total = ref[0]
        for k in range(1, count):
            total = total + ref[k]
        return total

    panel = panel_ref[...]
    gram = lax.dot_general(
        panel, panel, (((0,), (0,)), ((), ())), precision=HIGHEST, preferred_element_type=F32
    )
    gram_own[...] = gram.reshape(n_slab, part_rows, cols)
    exchange = slab_exchange(lambda peer: gram_own.at[peer], gram_scatter, 0)
    gram_scatter[me_s] = gram_own[me_s]

    line = iota((rows_dev, depth), 0)
    strip = iota((rows_dev, depth), 1) // INTERFACE_STRIP
    spread_map[...] = jnp.where(lax.rem(line, per_layer) == strip, 1.0, 0.0).astype(BF16)
    owner = iota((layers, rows_dev), 1) // per_layer == iota((layers, rows_dev), 0)
    guess = guess_ref[...]
    placed = jnp.where(owner, jnp.broadcast_to(guess, (layers, rows_dev)), 0.0)
    ghost = jnp.zeros((layers, depth), F32)
    for piece in split3(placed):
        ghost = ghost + jnp.dot(piece.astype(BF16), spread_map[...], preferred_element_type=F32)
    empty = jnp.zeros((1, depth), F32)
    for side in range(2):
        for x in range(layers):
            cells[side, x, TOP + height : TOP + height + 1, :] = ghost[x : x + 1, :]
            cells[side, x, TOP - 1 : TOP, :] = empty

    def march_plane(now, x, below, above):
        for y in range(0, height, 16):
            cells[1 - now, x, TOP + y : TOP + y + 16, :] = march_rows(
                cells[now, x, TOP + y : TOP + y + 16, :],
                above(y),
                below(y),
                cells[now, x, TOP + y + 1 : TOP + y + 17, :],
                cells[now, x, TOP + y - 1 : TOP + y + 15, :],
                rate[x, y : y + 16, :],
                [flow[d, x, y : y + 16, :] for d in range(3)],
            )

    def plane_of(now, x):
        return lambda y: cells[now, x, TOP + y : TOP + y + 16, :]

    def halo_of(sweep, side):
        return lambda y: halo[sweep, side, y : y + 16, :]

    for g in (0, 3):
        for c in loads[g]:
            c.wait()
    for sweep in range(SWEEPS):
        now = sweep % 2
        wait_halo(copies)
        march_plane(now, 0, halo_of(sweep, 0), plane_of(now, 1))
        march_plane(now, layers - 1, plane_of(now, layers - 2), halo_of(sweep, 1))
        if sweep < SWEEPS - 1:
            copies = halo_copies(
                sweep + 1,
                cells.at[1 - now, 0, pl.ds(TOP, height)],
                cells.at[1 - now, layers - 1, pl.ds(TOP, height)],
            )
            send_halo(copies)
        if sweep == 0:
            for g in (1, 2):
                for c in loads[g]:
                    c.wait()

        def interior(x, _):
            march_plane(now, x, plane_of(now, x - 1), plane_of(now, x + 1))
            return 0

        lax.fori_loop(1, layers - 1, interior, 0)
        if sweep == 0:
            finish(exchange)
            gram_sum[...] = summed(gram_scatter, n_slab)
            gram_wide[me_w] = gram_sum[...]
            exchange = wide_exchange(gram_sum, gram_wide, 0)
        elif sweep == 1:
            finish(exchange)
            gram_part[...] = summed(gram_wide, n_wide)
            gram_full[me_s] = gram_part[...]
            exchange = slab_exchange(lambda peer: gram_part, gram_full, 1)

    last = SWEEPS % 2
    store = pltpu.make_async_copy(
        cells.at[last, :, pl.ds(TOP, height)], final_hbm.at[0], store_sem
    )
    store.start()

    face_cells = jnp.concatenate(
        [cells[last, x, TOP + height - 1 : TOP + height, :] for x in range(layers)], axis=0
    )
    sums = jnp.zeros((layers, rows_dev), F32)
    for piece in split3(face_cells):
        sums = sums + lax.dot_general(
            piece.astype(BF16),
            spread_map[...],
            (((1,), (1,)), ((), ())),
            preferred_element_type=F32,
        )
    means = jnp.sum(jnp.where(owner, sums, 0.0), axis=0, keepdims=True) * (1.0 / INTERFACE_STRIP)
    face_own[...] = jnp.broadcast_to(means, (8, rows_dev))
    faces = []
    for k in range(n_slab):
        c = pltpu.make_async_remote_copy(
            src_ref=face_own,
            dst_ref=face_all.at[me_s],
            send_sem=face_send.at[k],
            recv_sem=face_recv.at[k],
            device_id=(across, slab_peer(k)),
            device_id_type=MESH,
        )
        c.start()
        faces.append(c)

    facing = rows_ref[...]
    for s in range(n_slab):
        picked = iota((rows_dev, rows_dev), 0) + s * rows_dev == jnp.broadcast_to(
            facing, (rows_dev, rows_dev)
        )
        pick_map[s] = jnp.where(picked, 1.0, 0.0).astype(BF16)

    finish(exchange)
    blocks = cols // 8
    square = gram_full[...].reshape(cols, cols)
    strips = [square[8 * t : 8 * t + 8, :] for t in range(blocks)]
    third = blocks // 3
    strips = eliminate(strips, 0, third, blocks)

    finish(faces)
    line8 = iota((8, rows_dev), 0)
    tilde = jnp.zeros((8, rows_dev), F32)
    for s in range(n_slab):
        hi, mid, low = split3(face_all[s])
        triple = jnp.where(line8 == 0, hi, jnp.where(line8 == 1, mid, low))
        triple = jnp.where(line8 < 3, triple, 0.0).astype(BF16)
        tilde = tilde + jnp.dot(triple, pick_map[s], preferred_element_type=F32)
    tilde = jnp.sum(tilde, axis=0, keepdims=True)
    resid = tilde - guess
    proj_own[...] = jnp.dot(
        jnp.broadcast_to(resid, (8, rows_dev)),
        panel_ref[...],
        precision=HIGHEST,
        preferred_element_type=F32,
    )
    proj_slab[me_s] = proj_own[...]
    exchange = slab_exchange(lambda peer: proj_own, proj_slab, 2)
    strips = eliminate(strips, third, 2 * third, blocks)
    finish(exchange)
    proj_sum[...] = summed(proj_slab, n_slab)
    proj_wide[me_w] = proj_sum[...]
    exchange = wide_exchange(proj_sum, proj_wide, 1)
    strips = eliminate(strips, 2 * third, blocks, blocks)

    for t in range(blocks):
        on_diagonal = iota((8, cols), 1) == iota((8, cols), 0) + 8 * t
        pivots = jnp.sum(jnp.where(on_diagonal, strips[t], 0.0), axis=1, keepdims=True)
        root = 1.0 / jnp.sqrt(jnp.broadcast_to(pivots, (8, cols)))
        elim[8 * t : 8 * t + 8, :] = jnp.where(on_diagonal, 1.0, strips[t]) * root
    inverse = elim[...]
    basis_ref[...] = math.sqrt(total_rows) * lax.dot_general(
        panel_ref[...],
        inverse,
        (((1,), (1,)), ((), ())),
        precision=HIGHEST,
        preferred_element_type=F32,
    )
    finish(exchange)
    projection = summed(proj_wide, n_wide)
    half = lax.dot_general(
        projection,
        inverse,
        (((1,), (1,)), ((), ())),
        precision=HIGHEST,
        preferred_element_type=F32,
    )
    coefficients = jnp.dot(half, inverse, precision=HIGHEST, preferred_element_type=F32)
    update = lax.dot_general(
        coefficients,
        output_ref[...],
        (((1,), (1,)), ((), ())),
        precision=HIGHEST,
        preferred_element_type=F32,
    )
    updated_ref[...] = tilde - update[:1, :]
    store.wait()


def shards(n_wide, n_slab, state, rate, flow, guess, rows, panel, output):
    _, layers, height, depth = state.shape
    rows_dev, cols = panel.shape[1:]
    part_rows = cols // n_slab
    dma = pltpu.SemaphoreType.DMA
    vmem = pl.BlockSpec(memory_space=pltpu.VMEM)
    hbm = pl.BlockSpec(memory_space=pl.ANY)
    final, updated, basis = pl.pallas_call(
        functools.partial(kernel, n_wide, n_slab, rows_dev * n_wide * n_slab),
        out_shape=(
            jax.ShapeDtypeStruct(state.shape, F32),
            jax.ShapeDtypeStruct(guess.shape, F32),
            jax.ShapeDtypeStruct(panel.shape[1:], F32),
        ),
        in_specs=[hbm, hbm, hbm, vmem, vmem, vmem, vmem],
        out_specs=(hbm, vmem, vmem),
        scratch_shapes=[
            pltpu.VMEM((2, layers, height + 2 * TOP, depth), F32),
            pltpu.VMEM((SWEEPS, 2, height, depth), F32),
            pltpu.VMEM((layers, height, depth), BF16),
            pltpu.VMEM((3, layers, height, depth), BF16),
            pltpu.VMEM((rows_dev, depth), BF16),
            pltpu.VMEM((n_slab, rows_dev, rows_dev), BF16),
            pltpu.VMEM((n_slab, part_rows, cols), F32),
            pltpu.VMEM((n_slab, part_rows, cols), F32),
            pltpu.VMEM((part_rows, cols), F32),
            pltpu.VMEM((n_wide, part_rows, cols), F32),
            pltpu.VMEM((part_rows, cols), F32),
            pltpu.VMEM((n_slab, part_rows, cols), F32),
            pltpu.VMEM((cols, cols), F32),
            pltpu.VMEM((8, rows_dev), F32),
            pltpu.VMEM((n_slab, 8, rows_dev), F32),
            pltpu.VMEM((8, cols), F32),
            pltpu.VMEM((n_slab, 8, cols), F32),
            pltpu.VMEM((8, cols), F32),
            pltpu.VMEM((n_wide, 8, cols), F32),
            dma((4, 3)),
            dma,
            dma((SWEEPS, 2)),
            dma((SWEEPS, 2)),
            dma((3, n_slab)),
            dma((3, n_slab)),
            dma((2, n_wide)),
            dma((2, n_wide)),
            dma((n_slab,)),
            dma((n_slab,)),
        ],
        compiler_params=pltpu.CompilerParams(
            collective_id=0, has_side_effects=True, vmem_limit_bytes=40 * 1024 * 1024
        ),
    )(state, rate, flow, guess, rows, panel[0], output[0])
    return final, updated, basis[None]


def solution(mesh):
    return jax.shard_map(
        functools.partial(shards, mesh.shape["wide"], mesh.shape["slab"]),
        mesh=mesh,
        in_specs=(
            P("wide", "slab", None, None),
            P("wide", "slab", None, None),
            P(None, "wide", "slab", None, None),
            P("wide", "slab"),
            P("wide", "slab"),
            P("wide", "slab", None),
            P("wide", "slab", None),
        ),
        out_specs=(P("wide", "slab", None, None), P("wide", "slab"), P("wide", "slab", None)),
        check_vma=False,
    )
```

time: 276 us -> 55.4 us (0.20)
  the two profiles are of different devices: /device:TPU:0 before, /device:TPU:1 now
where the time goes in v1:
time: 55.4 us; the launch traced here: 55.1 us
  Pallas kernels  44 us (79%)
  local copies, waits for them, and re-layouts  10.4 us (19%)
  between operations  0.66 us (1%)
    pallas_call x1, Pallas kernels, shards(): pl.pallas_call(functools.partial(kernel, n_wide, n_slab, rows_dev * n_wid...  44 us
    unnamed x17, local copies, waits for them, and re-layouts  10.4 us

profile of v1, /device:TPU:1, one launch (start us, length us, event | category | flops | bytes accessed | tf_op | source)
XLA Modules:
  0.0 55.1 jit_solution(18320390126013801555)
XLA Ops:
  0.6 0.0 copy-start
  0.6 1.9 %copy-done = bf16[3,1,16,32,1024]{4,3,2,1,0:T(8,128)(2,1)S(1)} copy-done((bf16[3,1,16,32,1024]{4,3,2,1,0:T(8,128)(2,1)S(1)}, bf16[3,1,16,32,1024]{4,3,2,1,0:T(8,128)(2,1)}, u32[]{:S(2)}) %copy-start) | copy-done | bytes 3145752
  2.5 0.0 copy-start.1
  2.5 1.6 %copy-done.1 = f32[1,16,32,1024]{3,2,1,0:T(8,128)S(1)} copy-done((f32[1,16,32,1024]{3,2,1,0:T(8,128)S(1)}, f32[1,16,32,1024]{3,2,1,0:T(8,128)}, u32[]{:S(2)}) %copy-start.1) | copy-done | bytes 2097176
  4.1 0.0 copy-start.2
  4.1 1.2 %copy-done.2 = bf16[1,16,32,1024]{3,2,1,0:T(8,128)(2,1)S(1)} copy-done((bf16[1,16,32,1024]{3,2,1,0:T(8,128)(2,1)S(1)}, bf16[1,16,32,1024]{3,2,1,0:T(8,128)(2,1)}, u32[]{:S(2)}) %copy-start.2) | copy-done | bytes 1048600
  5.3 0.0 copy-start.3
  5.3 0.9 %copy-done.3 = f32[1,256,128]{2,1,0:T(8,128)S(1)} copy-done((f32[1,256,128]{2,1,0:T(8,128)S(1)}, f32[1,256,128]{2,1,0:T(8,128)}, u32[]{:S(2)}) %copy-start.3) | copy-done | bytes 131096
  6.2 0.0 copy-start.4
  6.2 0.9 %copy-done.4 = f32[1,256,128]{2,1,0:T(8,128)S(1)} copy-done((f32[1,256,128]{2,1,0:T(8,128)S(1)}, f32[1,256,128]{2,1,0:T(8,128)}, u32[]{:S(2)}) %copy-start.4) | copy-done | bytes 131096
  7.1 0.0 copy-start.5
  7.2 0.7 %copy-done.5 = f32[1,256]{1,0:T(1,128)S(1)} copy-done((f32[1,256]{1,0:T(1,128)S(1)}, f32[1,256]{1,0:T(1,128)}, u32[]{:S(2)}) %copy-start.5) | copy-done | bytes 1048
  7.8 0.0 copy-start.6
  7.8 0.7 %copy-done.6 = s32[1,256]{1,0:T(1,128)S(1)} copy-done((s32[1,256]{1,0:T(1,128)S(1)}, s32[1,256]{1,0:T(1,128)}, u32[]{:S(2)}) %copy-start.6) | copy-done | bytes 1048
  8.5 44.0 %shard_map.94 = (f32[1,16,32,1024]{3,2,1,0:T(8,128)S(1)}, f32[1,256]{1,0:T(1,128)S(1)}, f32[256,128]{1,0:T(8,128)S(1)}) custom-call(f32[1,16,32,1024]{3,2,1,0:T(8,128)S(1)} %copy-done.1, bf16[1,16,32,1024]{3,2,1,0:T(8,128)(2,1)S(1)} %copy-done.2, bf16[3,1,16,32,1024]{4,3,2,1,0:T(8,128)(2,1)S(1)} %copy-done, f32[1,256]{1,0:T(1,128)S(1)} %copy-done.5, ...), custom_call_target="tpu_custom_call" | custom-call | tf_op jit(solution)/shard_map/pallas_call | solution.py:447
  52.6 1.3 %copy.13 = f32[1,16,32,1024]{3,2,1,0:T(8,128)} copy(f32[1,16,32,1024]{3,2,1,0:T(8,128)S(1)} %get-tuple-element.12) | data formatting | bytes 4194304
  53.9 0.6 %copy.14 = f32[1,256]{1,0:T(1,128)} copy(f32[1,256]{1,0:T(1,128)S(1)} %get-tuple-element.13) | data formatting | bytes 2048
  54.4 0.7 %copy.15 = f32[1,256,128]{2,1,0:T(8,128)} copy(f32[1,256,128]{2,1,0:T(8,128)S(1)} %bitcast.5) | data formatting | bytes 262144
Async XLA Ops:
  0.6 1.9 %copy-start = (bf16[3,1,16,32,1024]{4,3,2,1,0:T(8,128)(2,1)S(1)}, bf16[3,1,16,32,1024]{4,3,2,1,0:T(8,128)(2,1)}, u32[]{:S(2)}) copy-start(bf16[3,1,16,32,1024]{4,3,2,1,0:T(8,128)(2,1)} %flow_hbm.1) | copy-start | bytes 9437188
  2.5 1.6 %copy-start.1 = (f32[1,16,32,1024]{3,2,1,0:T(8,128)S(1)}, f32[1,16,32,1024]{3,2,1,0:T(8,128)}, u32[]{:S(2)}) copy-start(f32[1,16,32,1024]{3,2,1,0:T(8,128)} %state_hbm.1) | copy-start | bytes 6291460
  4.1 1.2 %copy-start.2 = (bf16[1,16,32,1024]{3,2,1,0:T(8,128)(2,1)S(1)}, bf16[1,16,32,1024]{3,2,1,0:T(8,128)(2,1)}, u32[]{:S(2)}) copy-start(bf16[1,16,32,1024]{3,2,1,0:T(8,128)(2,1)} %rate_hbm.1) | copy-start | bytes 3145732
  5.3 0.9 %copy-start.3 = (f32[1,256,128]{2,1,0:T(8,128)S(1)}, f32[1,256,128]{2,1,0:T(8,128)}, u32[]{:S(2)}) copy-start(f32[1,256,128]{2,1,0:T(8,128)} %param.12) | copy-start | bytes 393220
  6.2 0.9 %copy-start.4 = (f32[1,256,128]{2,1,0:T(8,128)S(1)}, f32[1,256,128]{2,1,0:T(8,128)}, u32[]{:S(2)}) copy-start(f32[1,256,128]{2,1,0:T(8,128)} %param.13) | copy-start | bytes 393220
  7.1 0.7 %copy-start.5 = (f32[1,256]{1,0:T(1,128)S(1)}, f32[1,256]{1,0:T(1,128)}, u32[]{:S(2)}) copy-start(f32[1,256]{1,0:T(1,128)} %guess_ref.1) | copy-start | bytes 3076
  7.8 0.7 %copy-start.6 = (s32[1,256]{1,0:T(1,128)S(1)}, s32[1,256]{1,0:T(1,128)}, u32[]{:S(2)}) copy-start(s32[1,256]{1,0:T(1,128)} %rows_ref.1) | copy-start | bytes 3076

commit v2 on v1

--- a/solution.py
+++ b/solution.py
@@ -29,55 +29,84 @@
     return hi, mid, rest - mid
 
 
-def march_rows(centre, plus_first, minus_first, plus_second, minus_second, rate, flow):
-    depth = centre.shape[1]
-    lane = iota((centre.shape[0], 128), 1)
-    right = pltpu.roll(centre, depth - 1, 1)
-    left = pltpu.roll(centre, 1, 1)
-    plus_third = jnp.concatenate(
-        [right[:, : depth - 128], jnp.where(lane == 127, 0.0, right[:, depth - 128 :])], axis=1
-    )
-    minus_third = jnp.concatenate(
-        [jnp.where(lane == 0, 0.0, left[:, :128]), left[:, 128:]], axis=1
-    )
-    spread = (
-        (plus_first + minus_first)
-        + (plus_second + minus_second)
-        + (plus_third + minus_third)
-        - 6.0 * centre
-    )
-    carried = (
-        flow[0].astype(F32) * (plus_first - minus_first)
-        + flow[1].astype(F32) * (plus_second - minus_second)
-        + flow[2].astype(F32) * (plus_third - minus_third)
-    )
-    return centre + (STEP_SIZE * rate.astype(F32) * spread - (0.5 * STEP_SIZE) * carried)
-
-
-def eliminate(strips, first, last, blocks):
+def march_rows(source, target, x, y, rate, flow):
+    depth = source.shape[2]
+    tiles = depth // 128
+    rows = pl.ds(TOP + y, 16)
+    lane = iota((16, 128), 1)
+
+    def at(c):
+        return pl.ds(c * 128, 128)
+
+    zero = jnp.zeros((16, 128), F32)
+    centre = source[x, rows, at(0)]
+    left_before, left, right = zero, pltpu.roll(centre, 1, 1), pltpu.roll(centre, 127, 1)
+    for c in range(tiles):
+        if c < tiles - 1:
+            after = source[x, rows, at(c + 1)]
+            left_after, right_after = pltpu.roll(after, 1, 1), pltpu.roll(after, 127, 1)
+        else:
+            after = left_after = right_after = zero
+        plus_third = jnp.where(lane == 127, right_after, right)
+        minus_third = jnp.where(lane == 0, left_before, left)
+        plus_first = source[x + 1, rows, at(c)]
+        minus_first = source[x - 1, rows, at(c)]
+        plus_second = source[x, TOP + y + 1 : TOP + y + 17, at(c)]
+        minus_second = source[x, TOP + y - 1 : TOP + y + 15, at(c)]
+        spread = (
+            (plus_first + minus_first)
+            + (plus_second + minus_second)
+            + (plus_third + minus_third)
+            - 6.0 * centre
+        )
+        here = (pl.ds(y, 16), at(c))
+        carried = (
+            flow[(0, x - 1) + here].astype(F32) * (plus_first - minus_first)
+            + flow[(1, x - 1) + here].astype(F32) * (plus_second - minus_second)
+            + flow[(2, x - 1) + here].astype(F32) * (plus_third - minus_third)
+        )
+        target[x, rows, at(c)] = centre + STEP_SIZE * (
+            rate[(x - 1,) + here].astype(F32) * spread - 0.5 * carried
+        )
+        left_before, left, right, centre = left, left_after, right_after, after
+
+
+def eliminate_block(strips, b):
+    blocks = len(strips)
     lane = iota((8, 128), 1)
     row = iota((8, 128), 0)
-
-    def block(b, strips):
-        strips = list(strips)
-        for i in range(8):
-            columns = [jnp.broadcast_to(s[:, i : i + 1], (8, 128)) for s in strips]
-            pivot = jnp.broadcast_to(columns[0][i : i + 1, :], (8, 128))
-            inverse = 1.0 / pivot
-            along = jnp.broadcast_to(strips[0][i : i + 1, :], (8, 128))
-            scaled = jnp.where(lane == i, inverse, along * inverse)
-            below = row > i
-            strips[0] = jnp.where((lane == i) & below, 0.0, strips[0]) - jnp.where(
-                below, columns[0], 0.0
-            ) * scaled
-            for t in range(1, blocks):
-                strips[t] = jnp.where(lane == i, 0.0, strips[t]) - columns[t] * scaled
-        kept = ((lane < 8) & (lane <= row)) | (lane >= 8 * (blocks - b))
-        strips[0] = jnp.where(kept, strips[0], 0.0)
-        strips = [pltpu.roll(s, 128 - 8, 1) for s in strips]
-        return tuple(strips[1:] + strips[:1])
-
-    return lax.fori_loop(first, last, block, tuple(strips))
+    strips = list(strips)
+
+    def column(s, i):
+        return jnp.broadcast_to(s[:, i : i + 1], (8, 128))
+
+    def line(s, i):
+        return jnp.broadcast_to(s[i : i + 1, :], (8, 128))
+
+    for i in range(0, 8, 2):
+        j = i + 1
+        first = [column(s, i) for s in strips]
+        second = [column(s, j) for s in strips]
+        row_i, row_j = line(strips[0], i), line(strips[0], j)
+        over = line(second[0], i)
+        inverse_i = 1.0 / line(first[0], i)
+        factor = line(first[0], j) * inverse_i
+        inverse_j = 1.0 / (line(second[0], j) - factor * over)
+        ratio = over * inverse_i
+        scaled_i = jnp.where(lane == i, inverse_i, jnp.where(lane == j, 0.0, row_i * inverse_i))
+        new_j = jnp.where(lane == i, -factor, row_j - factor * row_i)
+        scaled_j = jnp.where(lane == j, inverse_j, new_j * inverse_j)
+        pair = (lane == i) | (lane == j)
+        updated = [
+            jnp.where(pair, 0.0, s) - f * scaled_i - (g - f * ratio) * scaled_j
+            for s, f, g in zip(strips, first, second)
+        ]
+        updated[0] = jnp.where(row > j, updated[0], jnp.where(row == j, new_j, strips[0]))
+        strips = updated
+    kept = ((lane < 8) & (lane <= row)) | (lane >= 8 * (blocks - b))
+    strips[0] = jnp.where(kept, strips[0], 0.0)
+    strips = [pltpu.roll(s, 128 - 8, 1) for s in strips]
+    return tuple(strips[1:] + strips[:1])
 
 
 def kernel(
@@ -87,15 +116,19 @@
     state_hbm,
     rate_hbm,
     flow_hbm,
+    guess_hbm,
+    rows_hbm,
+    panel_hbm,
+    output_hbm,
+    final_hbm,
+    updated_ref,
+    basis_ref,
     guess_ref,
     rows_ref,
     panel_ref,
     output_ref,
-    final_hbm,
-    updated_ref,
-    basis_ref,
-    cells,
-    halo,
+    cells_a,
+    cells_b,
     rate,
     flow,
     spread_map,
@@ -114,6 +147,7 @@
     proj_sum,
     proj_wide,
     load_sem,
+    small_sem,
     store_sem,
     halo_send,
     halo_recv,
@@ -124,7 +158,7 @@
     face_send,
     face_recv,
 ):
-    layers, depth = cells.shape[1], cells.shape[3]
+    layers, depth = rate.shape[0], rate.shape[2]
     height = rate.shape[1]
     cols = panel_ref.shape[1]
     rows_dev = guess_ref.shape[1]
@@ -139,13 +173,28 @@
     def wide_peer(k):
         return lax.rem(me_w + k, n_wide)
 
+    small = [
+        pltpu.make_async_copy(source, target, small_sem.at[k])
+        for k, (source, target) in enumerate(
+            (
+                (panel_hbm.at[0], panel_ref),
+                (guess_hbm, guess_ref),
+                (rows_hbm, rows_ref),
+                (output_hbm.at[0], output_ref),
+            )
+        )
+    ]
+    for c in small:
+        c.start()
     quarter = layers // 4
     loads = {}
     for g in (0, 3, 1, 2):
         planes = pl.ds(g * quarter, quarter)
         loads[g] = [
             pltpu.make_async_copy(
-                state_hbm.at[0, planes], cells.at[0, planes, pl.ds(TOP, height)], load_sem.at[g, 0]
+                state_hbm.at[0, planes],
+                cells_a.at[pl.ds(1 + g * quarter, quarter), pl.ds(TOP, height)],
+                load_sem.at[g, 0],
             ),
             pltpu.make_async_copy(rate_hbm.at[0, planes], rate.at[planes], load_sem.at[g, 1]),
             pltpu.make_async_copy(
@@ -156,12 +205,13 @@
             c.start()
 
     zeros = jnp.zeros((height, depth), F32)
+    cells = (cells_a, cells_b)
     for side in range(2):
 
         @pl.when(me_s == side * (n_slab - 1))
         def _():
-            for sweep in range(SWEEPS):
-                halo[sweep, side] = zeros
+            for buffer in cells:
+                buffer[side * (layers + 1), TOP : TOP + height, :] = zeros
 
     barrier = pltpu.get_barrier_semaphore()
     peers = (
@@ -176,7 +226,7 @@
     def halo_copies(sweep, low, high):
         down = pltpu.make_async_remote_copy(
             src_ref=low,
-            dst_ref=halo.at[sweep, 1],
+            dst_ref=cells[sweep % 2].at[layers + 1, pl.ds(TOP, height)],
             send_sem=halo_send.at[sweep, 0],
             recv_sem=halo_recv.at[sweep, 1],
             device_id=(me_w, lax.max(me_s - 1, 0)),
@@ -184,7 +234,7 @@
         )
         up = pltpu.make_async_remote_copy(
             src_ref=high,
-            dst_ref=halo.at[sweep, 0],
+            dst_ref=cells[sweep % 2].at[0, pl.ds(TOP, height)],
             send_sem=halo_send.at[sweep, 1],
             recv_sem=halo_recv.at[sweep, 0],
             device_id=(me_w, lax.min(me_s + 1, n_slab - 1)),
@@ -255,6 +305,7 @@
             total = total + ref[k]
         return total
 
+    small[0].wait()
     panel = panel_ref[...]
     gram = lax.dot_general(
         panel, panel, (((0,), (0,)), ((), ())), precision=HIGHEST, preferred_element_type=F32
@@ -267,60 +318,53 @@
     strip = iota((rows_dev, depth), 1) // INTERFACE_STRIP
     spread_map[...] = jnp.where(lax.rem(line, per_layer) == strip, 1.0, 0.0).astype(BF16)
     owner = iota((layers, rows_dev), 1) // per_layer == iota((layers, rows_dev), 0)
+    small[1].wait()
     guess = guess_ref[...]
     placed = jnp.where(owner, jnp.broadcast_to(guess, (layers, rows_dev)), 0.0)
     ghost = jnp.zeros((layers, depth), F32)
     for piece in split3(placed):
         ghost = ghost + jnp.dot(piece.astype(BF16), spread_map[...], preferred_element_type=F32)
     empty = jnp.zeros((1, depth), F32)
-    for side in range(2):
+    for buffer in cells:
         for x in range(layers):
-            cells[side, x, TOP + height : TOP + height + 1, :] = ghost[x : x + 1, :]
-            cells[side, x, TOP - 1 : TOP, :] = empty
-
-    def march_plane(now, x, below, above):
-        for y in range(0, height, 16):
-            cells[1 - now, x, TOP + y : TOP + y + 16, :] = march_rows(
-                cells[now, x, TOP + y : TOP + y + 16, :],
-                above(y),
-                below(y),
-                cells[now, x, TOP + y + 1 : TOP + y + 17, :],
-                cells[now, x, TOP + y - 1 : TOP + y + 15, :],
-                rate[x, y : y + 16, :],
-                [flow[d, x, y : y + 16, :] for d in range(3)],
-            )
-
-    def plane_of(now, x):
-        return lambda y: cells[now, x, TOP + y : TOP + y + 16, :]
-
-    def halo_of(sweep, side):
-        return lambda y: halo[sweep, side, y : y + 16, :]
-
+            buffer[1 + x, TOP + height : TOP + height + 1, :] = ghost[x : x + 1, :]
+            buffer[1 + x, TOP - 1 : TOP, :] = empty
+
+    def march(sweep, x, ys):
+        for y in ys:
+            march_rows(cells[sweep % 2], cells[1 - sweep % 2], x, y, rate, flow)
+
+    every = range(0, height, 16)
+    blocks = cols // 8
+    strips = ()
     for g in (0, 3):
         for c in loads[g]:
             c.wait()
-    for sweep in range(SWEEPS):
-        now = sweep % 2
+    for sweep in range(SWEEPS - 1):
         wait_halo(copies)
-        march_plane(now, 0, halo_of(sweep, 0), plane_of(now, 1))
-        march_plane(now, layers - 1, plane_of(now, layers - 2), halo_of(sweep, 1))
-        if sweep < SWEEPS - 1:
-            copies = halo_copies(
-                sweep + 1,
-                cells.at[1 - now, 0, pl.ds(TOP, height)],
-                cells.at[1 - now, layers - 1, pl.ds(TOP, height)],
-            )
-            send_halo(copies)
+        march(sweep, 1, every)
+        march(sweep, layers, every)
+        copies = halo_copies(
+            sweep + 1,
+            cells[1 - sweep % 2].at[1, pl.ds(TOP, height)],
+            cells[1 - sweep % 2].at[layers, pl.ds(TOP, height)],
+        )
+        send_halo(copies)
         if sweep == 0:
             for g in (1, 2):
                 for c in loads[g]:
                     c.wait()
-
-        def interior(x, _):
-            march_plane(now, x, plane_of(now, x - 1), plane_of(now, x + 1))
-            return 0
-
-        lax.fori_loop(1, layers - 1, interior, 0)
+        if sweep == SWEEPS - 2:
+            finish(exchange)
+            square = gram_full[...].reshape(cols, cols)
+            strips = tuple(square[8 * t : 8 * t + 8, :] for t in range(blocks))
+
+        def interior(k, strips):
+            march(sweep, 2 + 2 * k, every)
+            march(sweep, 3 + 2 * k, every)
+            return eliminate_block(strips, k) if strips else strips
+
+        strips = lax.fori_loop(0, layers // 2 - 1, interior, strips)
         if sweep == 0:
             finish(exchange)
             gram_sum[...] = summed(gram_scatter, n_slab)
@@ -331,15 +375,21 @@
             gram_part[...] = summed(gram_wide, n_wide)
             gram_full[me_s] = gram_part[...]
             exchange = slab_exchange(lambda peer: gram_part, gram_full, 1)
+    done = layers // 2 - 1
+
+    wait_halo(copies)
+
+    def upper(k, strips):
+        for p in range(4):
+            march(SWEEPS - 1, 1 + 4 * k + p, every[1:])
+        return eliminate_block(strips, done + k)
+
+    strips = lax.fori_loop(0, layers // 4, upper, strips)
+    done += layers // 4
 
     last = SWEEPS % 2
-    store = pltpu.make_async_copy(
-        cells.at[last, :, pl.ds(TOP, height)], final_hbm.at[0], store_sem
-    )
-    store.start()
-
     face_cells = jnp.concatenate(
-        [cells[last, x, TOP + height - 1 : TOP + height, :] for x in range(layers)], axis=0
+        [cells[last][1 + x, TOP + height - 1 : TOP + height, :] for x in range(layers)], axis=0
     )
     sums = jnp.zeros((layers, rows_dev), F32)
     for piece in split3(face_cells):
@@ -364,19 +414,25 @@
         c.start()
         faces.append(c)
 
+    def lower(k, strips):
+        for p in range(4):
+            march(SWEEPS - 1, 1 + 4 * k + p, every[:1])
+        return eliminate_block(strips, done + k)
+
+    strips = lax.fori_loop(0, layers // 4, lower, strips)
+    done += layers // 4
+    store = pltpu.make_async_copy(
+        cells[last].at[pl.ds(1, layers), pl.ds(TOP, height)], final_hbm.at[0], store_sem
+    )
+    store.start()
+
+    small[2].wait()
     facing = rows_ref[...]
     for s in range(n_slab):
         picked = iota((rows_dev, rows_dev), 0) + s * rows_dev == jnp.broadcast_to(
             facing, (rows_dev, rows_dev)
         )
         pick_map[s] = jnp.where(picked, 1.0, 0.0).astype(BF16)
-
-    finish(exchange)
-    blocks = cols // 8
-    square = gram_full[...].reshape(cols, cols)
-    strips = [square[8 * t : 8 * t + 8, :] for t in range(blocks)]
-    third = blocks // 3
-    strips = eliminate(strips, 0, third, blocks)
 
     finish(faces)
     line8 = iota((8, rows_dev), 0)
@@ -396,12 +452,7 @@
     )
     proj_slab[me_s] = proj_own[...]
     exchange = slab_exchange(lambda peer: proj_own, proj_slab, 2)
-    strips = eliminate(strips, third, 2 * third, blocks)
-    finish(exchange)
-    proj_sum[...] = summed(proj_slab, n_slab)
-    proj_wide[me_w] = proj_sum[...]
-    exchange = wide_exchange(proj_sum, proj_wide, 1)
-    strips = eliminate(strips, 2 * third, blocks, blocks)
+    strips = lax.fori_loop(done, blocks, lambda b, s: eliminate_block(s, b), strips)
 
     for t in range(blocks):
         on_diagonal = iota((8, cols), 1) == iota((8, cols), 0) + 8 * t
@@ -409,6 +460,10 @@
         root = 1.0 / jnp.sqrt(jnp.broadcast_to(pivots, (8, cols)))
         elim[8 * t : 8 * t + 8, :] = jnp.where(on_diagonal, 1.0, strips[t]) * root
     inverse = elim[...]
+    finish(exchange)
+    proj_sum[...] = summed(proj_slab, n_slab)
+    proj_wide[me_w] = proj_sum[...]
+    exchange = wide_exchange(proj_sum, proj_wide, 1)
     basis_ref[...] = math.sqrt(total_rows) * lax.dot_general(
         panel_ref[...],
         inverse,
@@ -416,23 +471,20 @@
         precision=HIGHEST,
         preferred_element_type=F32,
     )
-    finish(exchange)
-    projection = summed(proj_wide, n_wide)
-    half = lax.dot_general(
-        projection,
+    small[3].wait()
+    turned = lax.dot_general(
         inverse,
-        (((1,), (1,)), ((), ())),
-        precision=HIGHEST,
-        preferred_element_type=F32,
-    )
-    coefficients = jnp.dot(half, inverse, precision=HIGHEST, preferred_element_type=F32)
-    update = lax.dot_general(
-        coefficients,
         output_ref[...],
         (((1,), (1,)), ((), ())),
         precision=HIGHEST,
         preferred_element_type=F32,
     )
+    response = lax.dot_general(
+        inverse, turned, (((0,), (0,)), ((), ())), precision=HIGHEST, preferred_element_type=F32
+    )
+    finish(exchange)
+    projection = summed(proj_wide, n_wide)
+    update = jnp.dot(projection, response, precision=HIGHEST, preferred_element_type=F32)
     updated_ref[...] = tilde - update[:1, :]
     store.wait()
 
@@ -443,7 +495,7 @@
     part_rows = cols // n_slab
     dma = pltpu.SemaphoreType.DMA
     vmem = pl.BlockSpec(memory_space=pltpu.VMEM)
-    hbm = pl.BlockSpec(memory_space=pl.ANY)
+    hbm = pl.BlockSpec(memory_space=pltpu.HBM)
     final, updated, basis = pl.pallas_call(
         functools.partial(kernel, n_wide, n_slab, rows_dev * n_wide * n_slab),
         out_shape=(
@@ -451,11 +503,15 @@
             jax.ShapeDtypeStruct(guess.shape, F32),
             jax.ShapeDtypeStruct(panel.shape[1:], F32),
         ),
-        in_specs=[hbm, hbm, hbm, vmem, vmem, vmem, vmem],
+        in_specs=[hbm] * 7,
         out_specs=(hbm, vmem, vmem),
         scratch_shapes=[
-            pltpu.VMEM((2, layers, height + 2 * TOP, depth), F32),
-            pltpu.VMEM((SWEEPS, 2, height, depth), F32),
+            pltpu.VMEM((1, rows_dev), F32),
+            pltpu.VMEM((1, rows_dev), jnp.int32),
+            pltpu.VMEM((rows_dev, cols), F32),
+            pltpu.VMEM((rows_dev, cols), F32),
+            pltpu.VMEM((layers + 2, height + 2 * TOP, depth), F32),
+            pltpu.VMEM((layers + 2, height + 2 * TOP, depth), F32),
             pltpu.VMEM((layers, height, depth), BF16),
             pltpu.VMEM((3, layers, height, depth), BF16),
             pltpu.VMEM((rows_dev, depth), BF16),
@@ -474,6 +530,7 @@
             pltpu.VMEM((8, cols), F32),
             pltpu.VMEM((n_wide, 8, cols), F32),
             dma((4, 3)),
+            dma((4,)),
             dma,
             dma((SWEEPS, 2)),
             dma((SWEEPS, 2)),
@@ -485,9 +542,9 @@
             dma((n_slab,)),
         ],
         compiler_params=pltpu.CompilerParams(
-            collective_id=0, has_side_effects=True, vmem_limit_bytes=40 * 1024 * 1024
+            collective_id=0, has_side_effects=True, vmem_limit_bytes=56 * 1024 * 1024
         ),
-    )(state, rate, flow, guess, rows, panel[0], output[0])
+    )(state, rate, flow, guess, rows, panel, output)
     return final, updated, basis[None]
 
 

time: 55.4 us -> 45.9 us (0.83)
  the two profiles are of different devices: /device:TPU:1 before, /device:TPU:0 now
where the time goes in v2:
time: 45.9 us; the launch traced here: 45.7 us
  Pallas kernels  40.7 us (89%)
  local copies, waits for them, and re-layouts  4.42 us (10%)
  between operations  0.66 us (1%)
    pallas_call x1, Pallas kernels, shards(): pl.pallas_call(functools.partial(kernel, n_wide, n_slab, rows_dev * n_wid...  40.7 us
    unnamed x7, local copies, waits for them, and re-layouts  4.42 us

profile of v2, /device:TPU:0, one launch (start us, length us, event | category | flops | bytes accessed | tf_op | source)
XLA Modules:
  0.0 45.7 jit_solution(5253766599314511200)
XLA Ops:
  0.6 40.7 %shard_map.94 = (f32[1,16,32,1024]{3,2,1,0:T(8,128)}, f32[1,256]{1,0:T(1,128)}, f32[256,128]{1,0:T(8,128)}) custom-call(f32[1,16,32,1024]{3,2,1,0:T(8,128)} %state_hbm.1, bf16[1,16,32,1024]{3,2,1,0:T(8,128)(2,1)} %rate_hbm.1, bf16[3,1,16,32,1024]{4,3,2,1,0:T(8,128)(2,1)} %flow_hbm.1, f32[1,256]{1,0:T(1,128)} %guess_hbm.1, s32[1,256]{1,0:T(1,128)} %rows_hbm.1, ...), custom_call_target="tpu_custom_call" | custom-call | tf_op jit(solution)/shard_map/pallas_call | solution.py:499
  41.3 0.0 copy-start.1
  41.3 0.0 copy-start
  41.3 3.2 %copy.13 = f32[1,16,32,1024]{3,2,1,0:T(8,128)} copy(f32[1,16,32,1024]{3,2,1,0:T(8,128)} %get-tuple-element.12) | data formatting | bytes 4194304
  44.5 0.0 copy-done.1
  44.5 0.6 %copy.14 = f32[1,256]{1,0:T(1,128)} copy(f32[1,256]{1,0:T(1,128)S(1)} %copy-done.1) | data formatting | bytes 2048
  45.1 0.0 copy-done
  45.1 0.7 %copy.15 = f32[1,256,128]{2,1,0:T(8,128)} copy(f32[1,256,128]{2,1,0:T(8,128)S(1)} %bitcast.1) | data formatting | bytes 262144
Async XLA Ops:
  41.3 3.2 %copy-start.1 = (f32[1,256]{1,0:T(1,128)S(1)}, f32[1,256]{1,0:T(1,128)}, u32[]{:S(2)}) copy-start(f32[1,256]{1,0:T(1,128)} %get-tuple-element.13) | copy-start | bytes 3076
  41.3 3.8 %copy-start = (f32[256,128]{1,0:T(8,128)S(1)}, f32[256,128]{1,0:T(8,128)}, u32[]{:S(2)}) copy-start(f32[256,128]{1,0:T(8,128)} %get-tuple-element.8) | copy-start | bytes 393220

commit v3 on v2

--- a/solution.py
+++ b/solution.py
@@ -29,7 +29,7 @@
     return hi, mid, rest - mid
 
 
-def march_rows(source, target, x, y, rate, flow):
+def march_rows(source, store, x, y, factors):
     depth = source.shape[2]
     tiles = depth // 128
     rows = pl.ds(TOP + y, 16)
@@ -59,15 +59,13 @@
             + (plus_third + minus_third)
             - 6.0 * centre
         )
-        here = (pl.ds(y, 16), at(c))
+        diffuse, first, second, third = factors(at(c))
         carried = (
-            flow[(0, x - 1) + here].astype(F32) * (plus_first - minus_first)
-            + flow[(1, x - 1) + here].astype(F32) * (plus_second - minus_second)
-            + flow[(2, x - 1) + here].astype(F32) * (plus_third - minus_third)
-        )
-        target[x, rows, at(c)] = centre + STEP_SIZE * (
-            rate[(x - 1,) + here].astype(F32) * spread - 0.5 * carried
-        )
+            first * (plus_first - minus_first)
+            + second * (plus_second - minus_second)
+            + third * (plus_third - minus_third)
+        )
+        store(at(c), centre + (diffuse * spread - carried))
         left_before, left, right, centre = left, left_after, right_after, after
 
 
@@ -120,7 +118,7 @@
     rows_hbm,
     panel_hbm,
     output_hbm,
-    final_hbm,
+    final_ref,
     updated_ref,
     basis_ref,
     guess_ref,
@@ -131,6 +129,7 @@
     cells_b,
     rate,
     flow,
+    scaled,
     spread_map,
     pick_map,
     gram_own,
@@ -148,7 +147,6 @@
     proj_wide,
     load_sem,
     small_sem,
-    store_sem,
     halo_send,
     halo_recv,
     slab_send,
@@ -314,16 +312,21 @@
     exchange = slab_exchange(lambda peer: gram_own.at[peer], gram_scatter, 0)
     gram_scatter[me_s] = gram_own[me_s]
 
-    line = iota((rows_dev, depth), 0)
-    strip = iota((rows_dev, depth), 1) // INTERFACE_STRIP
-    spread_map[...] = jnp.where(lax.rem(line, per_layer) == strip, 1.0, 0.0).astype(BF16)
-    owner = iota((layers, rows_dev), 1) // per_layer == iota((layers, rows_dev), 0)
+    line = lax.bitwise_and(iota((rows_dev, 1), 0), per_layer - 1)
+    strip = lax.shift_right_logical(iota((1, depth), 1), INTERFACE_STRIP.bit_length() - 1)
+    spread_map[...] = jnp.where(line == strip, 1.0, 0.0).astype(BF16)
+    owner = lax.shift_right_logical(
+        iota((layers, rows_dev), 1), per_layer.bit_length() - 1
+    ) == iota((layers, rows_dev), 0)
     small[1].wait()
     guess = guess_ref[...]
     placed = jnp.where(owner, jnp.broadcast_to(guess, (layers, rows_dev)), 0.0)
-    ghost = jnp.zeros((layers, depth), F32)
-    for piece in split3(placed):
-        ghost = ghost + jnp.dot(piece.astype(BF16), spread_map[...], preferred_element_type=F32)
+    pieces = jnp.dot(
+        jnp.concatenate(split3(placed), axis=0).astype(BF16),
+        spread_map[...],
+        preferred_element_type=F32,
+    )
+    ghost = pieces[:layers] + pieces[layers : 2 * layers] + pieces[2 * layers :]
     empty = jnp.zeros((1, depth), F32)
     for buffer in cells:
         for x in range(layers):
@@ -331,8 +334,27 @@
             buffer[1 + x, TOP - 1 : TOP, :] = empty
 
     def march(sweep, x, ys):
+        source, target = cells[sweep % 2], cells[1 - sweep % 2]
         for y in ys:
-            march_rows(cells[sweep % 2], cells[1 - sweep % 2], x, y, rate, flow)
+            rows = pl.ds(y, 16)
+
+            def factors(lanes):
+                if sweep:
+                    return [scaled[d, x - 1, rows, lanes] for d in range(4)]
+                found = [STEP_SIZE * rate[x - 1, rows, lanes].astype(F32)] + [
+                    (0.5 * STEP_SIZE) * flow[d, x - 1, rows, lanes].astype(F32) for d in range(3)
+                ]
+                for d in range(4):
+                    scaled[d, x - 1, rows, lanes] = found[d]
+                return found
+
+            def store(lanes, value):
+                if sweep == SWEEPS - 1:
+                    final_ref[0, x - 1, rows, lanes] = value
+                else:
+                    target[x, pl.ds(TOP + y, 16), lanes] = value
+
+            march_rows(source, store, x, y, factors)
 
     every = range(0, height, 16)
     blocks = cols // 8
@@ -354,8 +376,16 @@
             for g in (1, 2):
                 for c in loads[g]:
                     c.wait()
-        if sweep == SWEEPS - 2:
-            finish(exchange)
+        finish(exchange)
+        if sweep == 0:
+            gram_sum[...] = summed(gram_scatter, n_slab)
+            gram_wide[me_w] = gram_sum[...]
+            exchange = wide_exchange(gram_sum, gram_wide, 0)
+        elif sweep == 1:
+            gram_part[...] = summed(gram_wide, n_wide)
+            gram_full[me_s] = gram_part[...]
+            exchange = slab_exchange(lambda peer: gram_part, gram_full, 1)
+        else:
             square = gram_full[...].reshape(cols, cols)
             strips = tuple(square[8 * t : 8 * t + 8, :] for t in range(blocks))
 
@@ -365,40 +395,27 @@
             return eliminate_block(strips, k) if strips else strips
 
         strips = lax.fori_loop(0, layers // 2 - 1, interior, strips)
-        if sweep == 0:
-            finish(exchange)
-            gram_sum[...] = summed(gram_scatter, n_slab)
-            gram_wide[me_w] = gram_sum[...]
-            exchange = wide_exchange(gram_sum, gram_wide, 0)
-        elif sweep == 1:
-            finish(exchange)
-            gram_part[...] = summed(gram_wide, n_wide)
-            gram_full[me_s] = gram_part[...]
-            exchange = slab_exchange(lambda peer: gram_part, gram_full, 1)
     done = layers // 2 - 1
 
     wait_halo(copies)
 
-    def upper(k, strips):
-        for p in range(4):
-            march(SWEEPS - 1, 1 + 4 * k + p, every[1:])
-        return eliminate_block(strips, done + k)
-
-    strips = lax.fori_loop(0, layers // 4, upper, strips)
-    done += layers // 4
-
-    last = SWEEPS % 2
+    def upper(k, _):
+        march(SWEEPS - 1, 1 + 2 * k, every[1:])
+        march(SWEEPS - 1, 2 + 2 * k, every[1:])
+        return 0
+
+    lax.fori_loop(0, layers // 2, upper, 0)
+
     face_cells = jnp.concatenate(
-        [cells[last][1 + x, TOP + height - 1 : TOP + height, :] for x in range(layers)], axis=0
-    )
-    sums = jnp.zeros((layers, rows_dev), F32)
-    for piece in split3(face_cells):
-        sums = sums + lax.dot_general(
-            piece.astype(BF16),
-            spread_map[...],
-            (((1,), (1,)), ((), ())),
-            preferred_element_type=F32,
-        )
+        [final_ref[0, x, height - 1 : height, :] for x in range(layers)], axis=0
+    )
+    sums = lax.dot_general(
+        jnp.concatenate(split3(face_cells), axis=0).astype(BF16),
+        spread_map[...],
+        (((1,), (1,)), ((), ())),
+        preferred_element_type=F32,
+    )
+    sums = sums[:layers] + sums[layers : 2 * layers] + sums[2 * layers :]
     means = jnp.sum(jnp.where(owner, sums, 0.0), axis=0, keepdims=True) * (1.0 / INTERFACE_STRIP)
     face_own[...] = jnp.broadcast_to(means, (8, rows_dev))
     faces = []
@@ -414,18 +431,6 @@
         c.start()
         faces.append(c)
 
-    def lower(k, strips):
-        for p in range(4):
-            march(SWEEPS - 1, 1 + 4 * k + p, every[:1])
-        return eliminate_block(strips, done + k)
-
-    strips = lax.fori_loop(0, layers // 4, lower, strips)
-    done += layers // 4
-    store = pltpu.make_async_copy(
-        cells[last].at[pl.ds(1, layers), pl.ds(TOP, height)], final_hbm.at[0], store_sem
-    )
-    store.start()
-
     small[2].wait()
     facing = rows_ref[...]
     for s in range(n_slab):
@@ -433,6 +438,14 @@
             facing, (rows_dev, rows_dev)
         )
         pick_map[s] = jnp.where(picked, 1.0, 0.0).astype(BF16)
+
+    def lower(k, strips):
+        march(SWEEPS - 1, 1 + 2 * k, every[:1])
+        march(SWEEPS - 1, 2 + 2 * k, every[:1])
+        return eliminate_block(strips, done + k)
+
+    pairs = layers // 2
+    strips = lax.fori_loop(0, pairs // 3 + 1, lower, strips)
 
     finish(faces)
     line8 = iota((8, rows_dev), 0)
@@ -452,7 +465,13 @@
     )
     proj_slab[me_s] = proj_own[...]
     exchange = slab_exchange(lambda peer: proj_own, proj_slab, 2)
-    strips = lax.fori_loop(done, blocks, lambda b, s: eliminate_block(s, b), strips)
+    strips = lax.fori_loop(pairs // 3 + 1, 2 * (pairs // 3 + 1), lower, strips)
+    finish(exchange)
+    proj_sum[...] = summed(proj_slab, n_slab)
+    proj_wide[me_w] = proj_sum[...]
+    exchange = wide_exchange(proj_sum, proj_wide, 1)
+    strips = lax.fori_loop(2 * (pairs // 3 + 1), pairs, lower, strips)
+    strips = lax.fori_loop(done + pairs, blocks, lambda b, s: eliminate_block(s, b), strips)
 
     for t in range(blocks):
         on_diagonal = iota((8, cols), 1) == iota((8, cols), 0) + 8 * t
@@ -460,10 +479,6 @@
         root = 1.0 / jnp.sqrt(jnp.broadcast_to(pivots, (8, cols)))
         elim[8 * t : 8 * t + 8, :] = jnp.where(on_diagonal, 1.0, strips[t]) * root
     inverse = elim[...]
-    finish(exchange)
-    proj_sum[...] = summed(proj_slab, n_slab)
-    proj_wide[me_w] = proj_sum[...]
-    exchange = wide_exchange(proj_sum, proj_wide, 1)
     basis_ref[...] = math.sqrt(total_rows) * lax.dot_general(
         panel_ref[...],
         inverse,
@@ -486,7 +501,19 @@
     projection = summed(proj_wide, n_wide)
     update = jnp.dot(projection, response, precision=HIGHEST, preferred_element_type=F32)
     updated_ref[...] = tilde - update[:1, :]
-    store.wait()
+
+
+def put(final_ref, updated_ref, basis_ref, final_hbm, updated_hbm, basis_hbm, sem):
+    copies = [
+        pltpu.make_async_copy(source, target, sem.at[k])
+        for k, (source, target) in enumerate(
+            ((final_ref, final_hbm), (updated_ref, updated_hbm), (basis_ref, basis_hbm))
+        )
+    ]
+    for c in copies:
+        c.start()
+    for c in copies:
+        c.wait()
 
 
 def shards(n_wide, n_slab, state, rate, flow, guess, rows, panel, output):
@@ -504,7 +531,7 @@
             jax.ShapeDtypeStruct(panel.shape[1:], F32),
         ),
         in_specs=[hbm] * 7,
-        out_specs=(hbm, vmem, vmem),
+        out_specs=(vmem, vmem, vmem),
         scratch_shapes=[
             pltpu.VMEM((1, rows_dev), F32),
             pltpu.VMEM((1, rows_dev), jnp.int32),
@@ -514,6 +541,7 @@
             pltpu.VMEM((layers + 2, height + 2 * TOP, depth), F32),
             pltpu.VMEM((layers, height, depth), BF16),
             pltpu.VMEM((3, layers, height, depth), BF16),
+            pltpu.VMEM((4, layers, height, depth), F32),
             pltpu.VMEM((rows_dev, depth), BF16),
             pltpu.VMEM((n_slab, rows_dev, rows_dev), BF16),
             pltpu.VMEM((n_slab, part_rows, cols), F32),
@@ -531,7 +559,6 @@
             pltpu.VMEM((n_wide, 8, cols), F32),
             dma((4, 3)),
             dma((4,)),
-            dma,
             dma((SWEEPS, 2)),
             dma((SWEEPS, 2)),
             dma((3, n_slab)),
@@ -542,10 +569,23 @@
             dma((n_slab,)),
         ],
         compiler_params=pltpu.CompilerParams(
-            collective_id=0, has_side_effects=True, vmem_limit_bytes=56 * 1024 * 1024
+            collective_id=0, has_side_effects=True, vmem_limit_bytes=44 * 1024 * 1024
         ),
-    )(state, rate, flow, guess, rows, panel, output)
-    return final, updated, basis[None]
+    )(
+        *(
+            pltpu.with_memory_space_constraint(value, pltpu.HBM)
+            for value in (state, rate, flow, guess, rows, panel, output)
+        )
+    )
+    outs = (final, updated, basis[None])
+    return pl.pallas_call(
+        put,
+        out_shape=tuple(jax.ShapeDtypeStruct(o.shape, F32) for o in outs),
+        in_specs=[vmem] * 3,
+        out_specs=(hbm,) * 3,
+        scratch_shapes=[dma((3,))],
+        compiler_params=pltpu.CompilerParams(vmem_limit_bytes=16 * 1024 * 1024),
+    )(*outs)
 
 
 def solution(mesh):

time: 45.9 us -> 38.9 us (0.85)
  local copies, waits for them, and re-layouts: 4.42 us -> 0 us
  Pallas kernels: 40.7 us -> 38.1 us
    unnamed x7 -> x0, local copies, waits for them, and re-layouts: 4.42 us -> none
    pallas_call x1, Pallas kernels: 40.7 us -> 36.7 us  [shards(): pl.pallas_call(functools.partial(kernel, n_wide, n_slab, rows_dev * n_wid...]
    pallas_call x0 -> x1, Pallas kernels: none -> 1.38 us  [shards(): pl.pallas_call(put, out_shape=tuple((jax.ShapeDtypeStruct(o.shape, F32) f...]
where the time goes in v3:
time: 38.9 us; the launch traced here: 38.7 us
  Pallas kernels  38.1 us (98%)
  between operations  0.64 us (2%)
    pallas_call x1, Pallas kernels, shards(): pl.pallas_call(functools.partial(kernel, n_wide, n_slab, rows_dev * n_wid...  36.7 us
    pallas_call x1, Pallas kernels, shards(): pl.pallas_call(put, out_shape=tuple((jax.ShapeDtypeStruct(o.shape, F32) f...  1.38 us

profile of v3, /device:TPU:0, one launch (start us, length us, event | category | flops | bytes accessed | tf_op | source)
XLA Modules:
  0.0 38.7 jit_solution(18155864727249673631)
XLA Ops:
  0.6 36.7 %shard_map.94 = (f32[1,16,32,1024]{3,2,1,0:T(8,128)S(1)}, f32[1,256]{1,0:T(1,128)S(1)}, f32[256,128]{1,0:T(8,128)S(1)}) custom-call(f32[1,16,32,1024]{3,2,1,0:T(8,128)} %state_hbm.1, bf16[1,16,32,1024]{3,2,1,0:T(8,128)(2,1)} %rate_hbm.1, bf16[3,1,16,32,1024]{4,3,2,1,0:T(8,128)(2,1)} %flow_hbm.1, f32[1,256]{1,0:T(1,128)} %guess_hbm.1, s32[1,256]{1,0:T(1,128)} %rows_hbm.1, ...), custom_call_target="tpu_custom_call" | custom-call | tf_op jit(solution)/shard_map/pallas_call | solution.py:526
  37.3 1.4 %shard_map.95 = (f32[1,16,32,1024]{3,2,1,0:T(8,128)}, f32[1,256]{1,0:T(1,128)}, f32[1,256,128]{2,1,0:T(8,128)}) custom-call(f32[1,16,32,1024]{3,2,1,0:T(8,128)S(1)} %get-tuple-element.6.final_ref, f32[1,256]{1,0:T(1,128)S(1)} %get-tuple-element.7.updated_ref, f32[1,256,128]{2,1,0:T(8,128)S(1)} %bitcast.1), custom_call_target="tpu_custom_call" | custom-call | tf_op jit(solution)/shard_map/pallas_call | solution.py:581
